TPU v7x, 32 devices: a whole 2x2x4 slice. The times are simulated.
32 devices in a mesh: context: 16 (over z, x, core), tensor: 2 (over y).
Axes of the slice: x: 2, y: 2, z: 4, core: 2. Of those that a mesh axis runs over, the one named last changes fastest.
Arguments:
- query: bfloat16 [6144, 4096], P('context', 'tensor'), may hold values from -16 to 16
- keys: bfloat16 [6144, 1024], P('context', 'tensor'), may hold values from -16 to 16
- values: bfloat16 [6144, 1024], P('context', 'tensor'), may hold values from -6 to 6
- vert_cols: int32 [8, 16], P('tensor'), may hold values from 0 to 6080, as said below
- slash_off: int32 [8, 15], P('tensor'), may hold values from 1 to 48, as said below
- doc_ids: int32 [96], replicated, may hold values from 0 to 3, never falling along the last dimension, each value on 1 to 48 neighbouring positions
- out_weight: bfloat16 [4096, 4096], P('tensor'), may hold values from -0.09375 to 0.09375
Outputs:
- layer_out: bfloat16 [6144, 4096], P(('context', 'tensor'))
Inputs may be any that keep to these rules, and one draw needn't show every extreme that they name: `vert_cols`: within one kv head the columns are distinct multiples of 64; every head has column 0. `slash_off`: within one kv head the offsets are distinct. `doc_ids`: never falling along the blocks; one document spans 1 to 48 blocks.
All inputs are finite; a program needn't handle non-finite values.
Results may differ from a plain program's by a relative error of at most 0.009.
Values may be sent and summed in bfloat16 or wider, within the bound.
A program may use at most 192 MiB of HBM per device.

v0:
```python
import jax
import jax.numpy as jnp
from jax import lax
from jax.sharding import PartitionSpec as P

QH = 32
KVH = 8
HD = 128
BLOCK = 64
HOPS = 8


floor_score = -1e30


def shifted(value, axis, steps):
    count = lax.axis_size(axis)
    initial, last = (max(0, -steps), min(count, count - steps))
    return lax.ppermute(value, axis, [(source, source + steps) for source in range(initial, last)])


def per_device(query, keys, values, vert_cols, slash_off, doc_ids, out_weight):
    tok_rows = keys.shape[0]
    heads_kv = vert_cols.shape[0]
    group_size = QH // KVH
    blocks = tok_rows // BLOCK
    first_block = lax.axis_index("context") * blocks
    stacked = jnp.stack([keys, values], axis=1)
    moving = stacked
    earlier = []
    for hop_index in range(HOPS):
        moving = shifted(moving, "context", 1)
        earlier = [moving] + earlier
    extended = jnp.concatenate(earlier + [stacked], axis=0)
    ext_blocks = extended.reshape(-1, BLOCK, 2, heads_kv, HD)
    own_blocks = stacked.reshape(blocks, BLOCK, 2, heads_kv, HD)
    head_ids = jnp.arange(heads_kv, dtype=jnp.int32)[:, None]
    column_blocks = vert_cols // BLOCK
    local_index = column_blocks - first_block
    owned = (local_index >= 0) & (local_index < blocks)
    picked = own_blocks[jnp.clip(local_index, 0, blocks - 1), :, :, head_ids]
    contrib = jnp.where(owned[:, :, None, None, None], picked.astype(jnp.float32), 0.0)
    columns = lax.psum(contrib, "context").astype(jnp.bfloat16)
    column_keys = columns[:, :, :, 0]
    column_values = columns[:, :, :, 1]
    local_ids = jnp.arange(blocks, dtype=jnp.int32)
    query_block = first_block + local_ids
    query_doc = doc_ids[query_block]
    slash_key = query_block[None, :, None] - slash_off[:, None, :]
    slash_live = (slash_key >= 0) & (doc_ids[jnp.maximum(slash_key, 0)] == query_doc[None, :, None])
    slash_pos = HOPS * blocks + local_ids[None, :, None] - slash_off[:, None, :]
    on_slash = jnp.any(
        query_block[None, :, None, None] - column_blocks[:, None, :, None]
        == slash_off[:, None, None, :],
        axis=-1,
    )
    same_doc = doc_ids[column_blocks][:, None, :] == query_doc[None, :, None]
    column_live = (column_blocks[:, None, :] < query_block[None, :, None]) & jnp.logical_not(
        on_slash & same_doc
    )
    queries = query.reshape(blocks, BLOCK, heads_kv, group_size, HD)
    causal_mask = jnp.arange(BLOCK)[:, None] >= jnp.arange(BLOCK)[None, :]
    width = max((divisor for divisor in range(1, 5) if blocks % divisor == 0))
    scale = HD ** (-0.5)

    def attend(index):
        lead = index * width
        q_part = lax.dynamic_slice_in_dim(queries, lead, width, 0)
        diagonal = lax.dynamic_slice_in_dim(own_blocks, lead, width, 0)
        band_pos = lax.dynamic_slice_in_dim(slash_pos, lead, width, 1)
        band_live = jnp.swapaxes(lax.dynamic_slice_in_dim(slash_live, lead, width, 1), 0, 1)
        cols_live = jnp.swapaxes(lax.dynamic_slice_in_dim(column_live, lead, width, 1), 0, 1)
        band = ext_blocks[band_pos, :, :, head_ids[:, :, None]]
        score_diag = (
            jnp.einsum(
                "brghd,bcgd->bghrc", q_part, diagonal[:, :, 0], preferred_element_type=jnp.float32
            )
            * scale
        )
        score_diag = jnp.where(causal_mask, score_diag, floor_score)
        band_mask = band_live[:, :, None, None, :, None]
        score_band = (
            jnp.einsum(
                "brghd,gbncd->bghrnc",
                q_part,
                band[:, :, :, :, 0],
                preferred_element_type=jnp.float32,
            )
            * scale
        )
        score_band = jnp.where(band_mask, score_band, floor_score)
        cols_mask = cols_live[:, :, None, None, :, None]
        score_cols = (
            jnp.einsum(
                "brghd,gncd->bghrnc", q_part, column_keys, preferred_element_type=jnp.float32
            )
            * scale
        )
        score_cols = jnp.where(cols_mask, score_cols, floor_score)
        top = jnp.maximum(
            jnp.max(score_diag, axis=-1),
            jnp.maximum(jnp.max(score_band, axis=(-2, -1)), jnp.max(score_cols, axis=(-2, -1))),
        )
        weight_diag = jnp.where(causal_mask, jnp.exp(score_diag - top[..., None]), 0.0)
        weight_band = jnp.where(band_mask, jnp.exp(score_band - top[..., None, None]), 0.0)
        weight_cols = jnp.where(cols_mask, jnp.exp(score_cols - top[..., None, None]), 0.0)
        total = (
            jnp.sum(weight_diag, axis=-1)
            + jnp.sum(weight_band, axis=(-2, -1))
            + jnp.sum(weight_cols, axis=(-2, -1))
        )
        summed = jnp.einsum(
            "bghrc,bcgd->brghd",
            weight_diag.astype(jnp.bfloat16),
            diagonal[:, :, 1],
            preferred_element_type=jnp.float32,
        )
        summed = summed + jnp.einsum(
            "bghrnc,gbncd->brghd",
            weight_band.astype(jnp.bfloat16),
            band[:, :, :, :, 1],
            preferred_element_type=jnp.float32,
        )
        summed = summed + jnp.einsum(
            "bghrnc,gncd->brghd",
            weight_cols.astype(jnp.bfloat16),
            column_values,
            preferred_element_type=jnp.float32,
        )
        return (summed / jnp.transpose(total, (0, 3, 1, 2))[..., None]).astype(jnp.bfloat16)

    attended = lax.map(attend, jnp.arange(blocks // width, dtype=jnp.int32)).reshape(tok_rows, -1)
    return lax.psum_scatter(
        jnp.dot(attended, out_weight, preferred_element_type=jnp.float32).astype(jnp.bfloat16),
        "tensor",
        scatter_dimension=0,
        tiled=True,
    )


def solution(mesh):
    placed = (
        P("context", "tensor"),
        P("context", "tensor"),
        P("context", "tensor"),
        P("tensor", None),
        P("tensor", None),
        P(),
        P("tensor", None),
    )
    return jax.shard_map(
        per_device,
        mesh=mesh,
        in_specs=placed,
        out_specs=P(("context", "tensor"), None),
        check_vma=False,
    )
```

profile of v0, /device:TPU:27, one launch (start us, length us, event | category | flops | bytes accessed | tf_op | source)
XLA Modules:
  0.0 513.6 jit_solution(11996780795609861470)
XLA Ops:
  7.7 1.3 collective-permute-start
  9.0 3.1 collective-permute-done
  13.4 12.0 %collective-permute-done.1 = bf16[384,2,512]{2,0,1:T(8,128)(2,1)S(1)} collective-permute-done((bf16[384,2,512]{2,0,1:T(8,128)(2,1)S(1)}, bf16[384,2,512]{2,0,1:T(8,128)(2,1)S(1)}, u32[]{:S(2)}, u32[]{:S(2)}) %collective-permute-start.1) | collective-permute-done | bytes 786464 | tf_op jit(solution)/shard_map/ppermute | solution.py:19
  26.7 12.0 %collective-permute-done.2 = bf16[384,2,512]{2,0,1:T(8,128)(2,1)S(1)} collective-permute-done((bf16[384,2,512]{2,0,1:T(8,128)(2,1)S(1)}, bf16[384,2,512]{2,0,1:T(8,128)(2,1)S(1)}, u32[]{:S(2)}, u32[]{:S(2)}) %collective-permute-start.2) | collective-permute-done | bytes 786464 | tf_op jit(solution)/shard_map/ppermute | solution.py:19
  43.0 9.1 %collective-permute-done.3 = bf16[384,2,512]{2,0,1:T(8,128)(2,1)} collective-permute-done((bf16[384,2,512]{2,0,1:T(8,128)(2,1)S(1)}, bf16[384,2,512]{2,0,1:T(8,128)(2,1)}, u32[]{:S(2)}, u32[]{:S(2)}) %collective-permute-start.3) | collective-permute-done | bytes 786464 | tf_op jit(solution)/shard_map/ppermute | solution.py:19
  54.6 2.3 copy_select_fusion
  56.9 8.8 %collective-permute-done.4 = bf16[384,2,512]{2,0,1:T(8,128)(2,1)} collective-permute-done((bf16[384,2,512]{2,0,1:T(8,128)(2,1)}, bf16[384,2,512]{2,0,1:T(8,128)(2,1)}, u32[]{:S(2)}, u32[]{:S(2)}) %collective-permute-start.4) | collective-permute-done | bytes 786464 | tf_op jit(solution)/shard_map/ppermute | solution.py:19
  67.0 113.8 %all-reduce.1 = bf16[4,16,64,2,128]{4,2,1,0,3:T(8,128)(2,1)} all-reduce(f32[4,16,64,2,128]{4,2,1,0,3:T(8,128)} %copy_select_fusion), channel_id=1, replica_groups=mesh['context'=16,'tensor'=2] {'context'}, use_global_device_ids=true, to_apply=%region_1.2 | all-reduce | flops 1048576 | bytes 6291456 | tf_op jit(solution)/shard_map/psum | solution.py:43
  181.2 2.7 gather_fusion.1
  184.0 1.3 collective-permute-start.6
  186.3 3.3 collective-permute-done.6
  190.9 2.4 reshape.93
  194.3 2.9 slice_bitcast_fusion
  197.2 6.0 %collective-permute-done.7 = bf16[384,2,512]{2,0,1:T(8,128)(2,1)} collective-permute-done((bf16[384,2,512]{2,0,1:T(8,128)(2,1)}, bf16[384,2,512]{2,0,1:T(8,128)(2,1)}, u32[]{:S(2)}, u32[]{:S(2)}) %collective-permute-start.7) | collective-permute-done | bytes 786464 | tf_op jit(solution)/shard_map/ppermute | solution.py:19
  203.2 2.1 constant_dynamic-update-slice_fusion.8
  205.3 2.1 constant_dynamic-update-slice_fusion.7
  208.3 2.1 constant_dynamic-update-slice_fusion.5
  210.4 2.1 constant_dynamic-update-slice_fusion.4
  216.3 12.8 %reshape.94 = bf16[54,64,2,4,128]{4,3,1,0,2:T(4,128)(2,1)} reshape(bf16[3456,2,512]{2,0,1:T(8,128)(2,1)} %constant_dynamic-update-slice_fusion) | data formatting | bytes 14155776 | tf_op jit(solution)/shard_map/reshape | solution.py:35
  229.1 8.1 %copy.94 = bf16[54,64,2,4,128]{4,1,3,2,0:T(8,128)(2,1)} copy(bf16[54,64,2,4,128]{4,3,1,0,2:T(4,128)(2,1)} %reshape.94) | data formatting | bytes 14155776
  237.2 200.4 %while.12 = (s32[]{:T(128)}, bf16[2,3,64,4,4,128]{5,4,3,2,1,0:T(4,128)(2,1)}, s32[2]{0:T(128)S(1)}, bf16[6,64,2,4,128]{4,1,3,2,0:T(8,128)(2,1)S(1)}, bf16[6,64,4...) while((s32[]{:T(128)}, ...), condition=%wide.region_9.10_spmd.clone.clone, body=%wide.region_2.9_spmd.clone.clone.sunk | while | flops 3291216896 | bytes 138418800 | solution.py:132
  238.5 1.4 constant_dynamic-slice_fusion.5
  239.9 10.6 %fusion.99 = (f32[3,4,4,64]{3,2,0,1:T(4,128)S(1)}, f32[4,3,64,4,16,64]{2,5,4,3,1,0:T(8,128)}) fusion(pred[3,4,16]{2,0,1:T(4,128)(4,1)S(1)} %bitcast.212, bf16[4,16,64,128]{3,2,1,0:T(8,128)(2,1)S(1)} %get-tuple-element.352, bf16[3,64,4,4,128]{4,3,2,1,0:T(4,128)(2,1)S(1)} %constant_dynamic-slice_fusion.5), kind=kOutput, calls=%fused_computation.14.clone.1 | convolution fusion | flops 814740480 | bytes 14430400 | tf_op jit(solution)/shard_map/while/body/eval_jaxpr/brghd,gncd->bghrnc/dot_general | solution.py:94
  250.6 1.8 fusion.100
  252.6 15.2 %gather_fusion = bf16[180,64,2,128]{3,1,2,0:T(8,128)(2,1)} fusion(bf16[54,64,2,4,128]{4,1,3,2,0:T(8,128)(2,1)} %get-tuple-element.350, s32[180]{0:T(256)S(1)} %reshape.166), kind=kCustom, calls=%fused_computation.clone.clone.1 | custom fusion | bytes 11797920 | tf_op jit(solution)/shard_map/while/body/eval_jaxpr/gather | solution.py:73
  267.8 5.8 %fusion.103 = (bf16[4,3,15,64,1,128]{5,3,4,2,1,0:T(8,128)(2,1)}, bf16[4,3,15,64,1,128]{5,3,4,2,1,0:T(8,128)(2,1)S(1)}) fusion(bf16[4,3,15,64,2,128]{5,3,4,2,1,0:T(8,128)(2,1)} %bitcast.206), kind=kLoop, calls=%fused_computation.119.clone.1 | loop fusion | bytes 11796480 | tf_op jit(solution)/shard_map/while/body/eval_jaxpr/slice | solution.py:121
  273.5 10.1 %bitcast_reduce_fusion.2 = (f32[3,4,4,64]{3,2,1,0:T(4,128)S(1)}, f32[3,4,15,64,64,4]{4,3,5,2,1,0:T(8,128)}) fusion(pred[3,4,15]{2,1,0:T(4,128)(4,1)S(1)} %dynamic-slice_bitcast_fusion.8, bf16[3,64,4,4,128]{4,3,2,1,0:T(4,128)(2,1)S(1)} %constant_dynamic-slice_fusion.5, bf16[4,3,15,64,1,128]{5,3,4,2,1,0:T(8,128)(2,1)S(1)} %get-tuple-element.303), kind=kOutput, calls=%fused_computation.10.clone.1 | convolution fusion | flops 763819008 | bytes 15544500 | tf_op jit(solution)/shard_map/while/body/eval_jaxpr/brghd,gbncd->bghrnc/dot_general | solution.py:83
  283.7 17.0 %fusion.105 = (f32[3,4,4,64]{3,2,0,1:T(4,128)S(1)}, bf16[3,4,4,64,16,64]{3,5,4,2,0,1:T(8,128)(2,1)}) fusion(f32[4,3,64,4,16,64]{2,5,4,3,1,0:T(8,128)} %get-tuple-element.301, pred[3,4,16]{2,0,1:T(4,128)(4,1)S(1)} %bitcast.213, f32[3,4,4,64]{3,2,1,0:T(4,128)S(1)} %fusion.104), kind=kLoop, calls=%fused_computation.15.clone.1 | loop fusion | flops 18871296 | bytes 18899136 | tf_op jit(solution)/shard_map/while/body/eval_jaxpr/reduce_sum | solution.py:110
  300.6 9.5 %fusion.106 = f32[4,3,4,64,128,1]{4,3,5,2,0,1:T(8,128)} fusion(bf16[3,4,4,64,16,64]{3,5,4,2,0,1:T(8,128)(2,1)} %get-tuple-element.306, bf16[4,16,64,128]{3,2,1,0:T(8,128)(2,1)} %get-tuple-element.353), kind=kOutput, calls=%fused_computation.19.clone.1 | convolution fusion | flops 805306368 | bytes 8912896 | tf_op jit(solution)/shard_map/while/body/eval_jaxpr/bghrnc,gncd->brghd/dot_general | solution.py:124
  310.1 1.4 fusion.107
  312.0 12.2 %fusion.109 = f32[3,4,4,64]{3,2,1,0:T(4,128)S(1)} fusion(f32[3,4,15,64,64,4]{4,3,5,2,1,0:T(8,128)} %get-tuple-element.308, f32[3,4,4,64]{3,2,1,0:T(4,128)S(1)} %fusion.104, pred[3,4,15]{2,1,0:T(4,128)(4,1)S(1)} %dynamic-slice_bitcast_fusion.8), kind=kLoop, calls=%fused_computation.17.clone.1 | loop fusion | flops 14742528 | bytes 11821236 | tf_op jit(solution)/shard_map/while/body/eval_jaxpr/reduce_sum | solution.py:109
  324.2 11.7 %fusion.111 = bf16[1,3,64,4,4,128]{5,2,4,3,1,0:T(8,128)(2,1)S(1)} fusion(f32[4,3,4,64,128,1]{4,3,5,2,0,1:T(8,128)} %fusion.106, f32[3,4,128,4,64]{2,4,3,1,0:T(8,128)S(1)} %fusion.107, f32[3,4,15,64,64,4]{4,3,5,2,1,0:T(8,128)} %get-tuple-element.308, f32[3,4,4,64]{3,2,1,0:T(4,128)S(1)} %fusion.104, ...), kind=kOutput, calls=%fused_computation.35.clone.1 | convolution fusion | flops 771293184 | bytes 18702516 | tf_op jit(solution)/shard_map/while/body/eval_jaxpr/bghrnc,gbncd->brghd/dot_general | solution.py:118
  335.9 1.5 copy_dynamic-update-slice_fusion.4
  338.7 1.4 constant_dynamic-slice_fusion.5
  340.1 10.6 %fusion.99 = (f32[3,4,4,64]{3,2,0,1:T(4,128)S(1)}, f32[4,3,64,4,16,64]{2,5,4,3,1,0:T(8,128)}) fusion(pred[3,4,16]{2,0,1:T(4,128)(4,1)S(1)} %bitcast.212, bf16[4,16,64,128]{3,2,1,0:T(8,128)(2,1)S(1)} %get-tuple-element.352, bf16[3,64,4,4,128]{4,3,2,1,0:T(4,128)(2,1)S(1)} %constant_dynamic-slice_fusion.5), kind=kOutput, calls=%fused_computation.14.clone.1 | convolution fusion | flops 814740480 | bytes 14430400 | tf_op jit(solution)/shard_map/while/body/eval_jaxpr/brghd,gncd->bghrnc/dot_general | solution.py:94
  350.8 1.8 fusion.100
  352.8 15.2 %gather_fusion = bf16[180,64,2,128]{3,1,2,0:T(8,128)(2,1)} fusion(bf16[54,64,2,4,128]{4,1,3,2,0:T(8,128)(2,1)} %get-tuple-element.350, s32[180]{0:T(256)S(1)} %reshape.166), kind=kCustom, calls=%fused_computation.clone.clone.1 | custom fusion | bytes 11797920 | tf_op jit(solution)/shard_map/while/body/eval_jaxpr/gather | solution.py:73
  368.0 5.8 %fusion.103 = (bf16[4,3,15,64,1,128]{5,3,4,2,1,0:T(8,128)(2,1)}, bf16[4,3,15,64,1,128]{5,3,4,2,1,0:T(8,128)(2,1)S(1)}) fusion(bf16[4,3,15,64,2,128]{5,3,4,2,1,0:T(8,128)(2,1)} %bitcast.206), kind=kLoop, calls=%fused_computation.119.clone.1 | loop fusion | bytes 11796480 | tf_op jit(solution)/shard_map/while/body/eval_jaxpr/slice | solution.py:121
  373.7 10.1 %bitcast_reduce_fusion.2 = (f32[3,4,4,64]{3,2,1,0:T(4,128)S(1)}, f32[3,4,15,64,64,4]{4,3,5,2,1,0:T(8,128)}) fusion(pred[3,4,15]{2,1,0:T(4,128)(4,1)S(1)} %dynamic-slice_bitcast_fusion.8, bf16[3,64,4,4,128]{4,3,2,1,0:T(4,128)(2,1)S(1)} %constant_dynamic-slice_fusion.5, bf16[4,3,15,64,1,128]{5,3,4,2,1,0:T(8,128)(2,1)S(1)} %get-tuple-element.303), kind=kOutput, calls=%fused_computation.10.clone.1 | convolution fusion | flops 763819008 | bytes 15544500 | tf_op jit(solution)/shard_map/while/body/eval_jaxpr/brghd,gbncd->bghrnc/dot_general | solution.py:83
  383.9 17.0 %fusion.105 = (f32[3,4,4,64]{3,2,0,1:T(4,128)S(1)}, bf16[3,4,4,64,16,64]{3,5,4,2,0,1:T(8,128)(2,1)}) fusion(f32[4,3,64,4,16,64]{2,5,4,3,1,0:T(8,128)} %get-tuple-element.301, pred[3,4,16]{2,0,1:T(4,128)(4,1)S(1)} %bitcast.213, f32[3,4,4,64]{3,2,1,0:T(4,128)S(1)} %fusion.104), kind=kLoop, calls=%fused_computation.15.clone.1 | loop fusion | flops 18871296 | bytes 18899136 | tf_op jit(solution)/shard_map/while/body/eval_jaxpr/reduce_sum | solution.py:110
  400.9 9.5 %fusion.106 = f32[4,3,4,64,128,1]{4,3,5,2,0,1:T(8,128)} fusion(bf16[3,4,4,64,16,64]{3,5,4,2,0,1:T(8,128)(2,1)} %get-tuple-element.306, bf16[4,16,64,128]{3,2,1,0:T(8,128)(2,1)} %get-tuple-element.353), kind=kOutput, calls=%fused_computation.19.clone.1 | convolution fusion | flops 805306368 | bytes 8912896 | tf_op jit(solution)/shard_map/while/body/eval_jaxpr/bghrnc,gncd->brghd/dot_general | solution.py:124
  410.3 1.4 fusion.107
  412.2 12.2 %fusion.109 = f32[3,4,4,64]{3,2,1,0:T(4,128)S(1)} fusion(f32[3,4,15,64,64,4]{4,3,5,2,1,0:T(8,128)} %get-tuple-element.308, f32[3,4,4,64]{3,2,1,0:T(4,128)S(1)} %fusion.104, pred[3,4,15]{2,1,0:T(4,128)(4,1)S(1)} %dynamic-slice_bitcast_fusion.8), kind=kLoop, calls=%fused_computation.17.clone.1 | loop fusion | flops 14742528 | bytes 11821236 | tf_op jit(solution)/shard_map/while/body/eval_jaxpr/reduce_sum | solution.py:109
  424.4 11.7 %fusion.111 = bf16[1,3,64,4,4,128]{5,2,4,3,1,0:T(8,128)(2,1)S(1)} fusion(f32[4,3,4,64,128,1]{4,3,5,2,0,1:T(8,128)} %fusion.106, f32[3,4,128,4,64]{2,4,3,1,0:T(8,128)S(1)} %fusion.107, f32[3,4,15,64,64,4]{4,3,5,2,1,0:T(8,128)} %get-tuple-element.308, f32[3,4,4,64]{3,2,1,0:T(4,128)S(1)} %fusion.104, ...), kind=kOutput, calls=%fused_computation.35.clone.1 | convolution fusion | flops 771293184 | bytes 18702516 | tf_op jit(solution)/shard_map/while/body/eval_jaxpr/bghrnc,gbncd->brghd/dot_general | solution.py:118
  436.1 1.5 copy_dynamic-update-slice_fusion.4
  437.6 2.9 reshape.95
  440.5 11.5 %convolution_convert_fusion = bf16[384,4096]{1,0:T(8,128)(2,1)} fusion(bf16[384,2048]{1,0:T(8,128)(2,1)S(1)} %reshape.95, bf16[2048,4096]{1,0:T(8,128)(2,1)} %param.15), kind=kOutput, calls=%fused_computation.75 | convolution fusion | flops 6444023808 | bytes 21495808 | tf_op jit(solution)/shard_map/dot_general | solution.py:134
  452.0 54.8 %reduce-scatter.2.cloned.1.call-done = bf16[192,4096]{1,0:T(8,128)(2,1)} async-done(((bf16[384,4096]{1,0:T(8,128)(2,1)}), bf16[192,4096]{1,0:T(8,128)(2,1)}) %reduce-scatter.2.cloned.1.call-update) | async-done | bytes 1572880 | tf_op jit(solution)/shard_map/reduce_scatter | solution.py:133
  (107 shorter events, 22.9 us)
Async XLA Ops:
  6.5 174.7 %copy-start = (s32[96]{0:T(128)S(1)}, s32[96]{0:T(128)}, u32[]{:S(2)}) copy-start(s32[96]{0:T(128)} %param.14) | copy-start | bytes 1156
  6.5 500.2 %reduce-scatter.2.cloned.1.call-start = ((), (), s32[]{:S(2)}) async-start(), calls=%async_computation.1 | async-start | bytes 4718592 | tf_op jit(solution)/shard_map/reduce_scatter | solution.py:133
  7.7 4.4 collective-permute-start
  12.1 26.6 %copy-start.8 = (bf16[384,2,512]{2,0,1:T(8,128)(2,1)}, bf16[384,2,512]{2,0,1:T(8,128)(2,1)S(1)}, u32[]{:S(2)}) copy-start(bf16[384,2,512]{2,0,1:T(8,128)(2,1)S(1)} %collective-permute-done) | copy-start | bytes 2359300
  12.1 13.3 %collective-permute-start.1 = (bf16[384,2,512]{2,0,1:T(8,128)(2,1)S(1)}, bf16[384,2,512]{2,0,1:T(8,128)(2,1)S(1)}, u32[]{:S(2)}, u32[]{:S(2)}) collective-permute-start(bf16[384,2,512]{2,0,1:T(8,128)(2,1)S(1)} %collective-permute-done), channel_id=1, source_target_pairs={{0,2},{2,4},{4,6},{6,8},{8,10},{10,12},{12,14},{14,16},{16,18},{18... | collective-permute-start | bytes 2359304 | tf_op jit(solution)/shard_map/ppermute | solution.py:19
  25.4 13.3 %copy-start.10 = (bf16[384,2,512]{2,0,1:T(8,128)(2,1)}, bf16[384,2,512]{2,0,1:T(8,128)(2,1)S(1)}, u32[]{:S(2)}) copy-start(bf16[384,2,512]{2,0,1:T(8,128)(2,1)S(1)} %collective-permute-done.1) | copy-start | bytes 2359300
  25.4 13.3 %collective-permute-start.2 = (bf16[384,2,512]{2,0,1:T(8,128)(2,1)S(1)}, bf16[384,2,512]{2,0,1:T(8,128)(2,1)S(1)}, u32[]{:S(2)}, u32[]{:S(2)}) collective-permute-start(bf16[384,2,512]{2,0,1:T(8,128)(2,1)S(1)} %collective-permute-done.1), channel_id=1, source_target_pairs={{0,2},{2,4},{4,6},{6,8},{8,10},{10,12},{12,14},{14,16},{16,18},{18... | collective-permute-start | bytes 2359304 | tf_op jit(solution)/shard_map/ppermute | solution.py:19
  38.7 13.4 %copy-start.12 = (bf16[384,2,512]{2,0,1:T(8,128)(2,1)}, bf16[384,2,512]{2,0,1:T(8,128)(2,1)S(1)}, u32[]{:S(2)}) copy-start(bf16[384,2,512]{2,0,1:T(8,128)(2,1)S(1)} %collective-permute-done.2) | copy-start | bytes 2359300
  38.7 13.4 %collective-permute-start.3 = (bf16[384,2,512]{2,0,1:T(8,128)(2,1)S(1)}, bf16[384,2,512]{2,0,1:T(8,128)(2,1)}, u32[]{:S(2)}, u32[]{:S(2)}) collective-permute-start(bf16[384,2,512]{2,0,1:T(8,128)(2,1)S(1)} %collective-permute-done.2), channel_id=1, source_target_pairs={{0,2},{2,4},{4,6},{6,8},{8,10},{10,12},{12,14},{14,16},{16,18},{18... | collective-permute-start | bytes 2359304 | tf_op jit(solution)/shard_map/ppermute | solution.py:19
  52.1 13.6 %collective-permute-start.4 = (bf16[384,2,512]{2,0,1:T(8,128)(2,1)}, bf16[384,2,512]{2,0,1:T(8,128)(2,1)}, u32[]{:S(2)}, u32[]{:S(2)}) collective-permute-start(bf16[384,2,512]{2,0,1:T(8,128)(2,1)} %collective-permute-done.3), channel_id=1, source_target_pairs={{0,2},{2,4},{4,6},{6,8},{8,10},{10,12},{12,14},{14,16},{16,18},{18... | collective-permute-start | bytes 2359304 | tf_op jit(solution)/shard_map/ppermute | solution.py:19
  54.6 126.3 %copy-start.16 = (s32[4,15]{1,0:T(4,128)S(1)}, s32[4,15]{1,0:T(4,128)}, u32[]{:S(2)}) copy-start(s32[4,15]{1,0:T(4,128)} %param.13) | copy-start | bytes 724
  65.8 118.3 %collective-permute-start.5 = (bf16[384,2,512]{2,0,1:T(8,128)(2,1)}, bf16[384,2,512]{2,0,1:T(8,128)(2,1)S(1)}, u32[]{:S(2)}, u32[]{:S(2)}) collective-permute-start(bf16[384,2,512]{2,0,1:T(8,128)(2,1)} %collective-permute-done.4), channel_id=1, source_target_pairs={{0,2},{2,4},{4,6},{6,8},{8,10},{10,12},{12,14},{14,16},{16,18},{18... | collective-permute-start | bytes 2359304 | tf_op jit(solution)/shard_map/ppermute | solution.py:19
  181.2 9.7 %copy-start.7 = (bf16[384,2048]{1,0:T(8,128)(2,1)S(1)}, bf16[384,2048]{1,0:T(8,128)(2,1)}, u32[]{:S(2)}) copy-start(bf16[384,2048]{1,0:T(8,128)(2,1)} %param.9) | copy-start | bytes 4718596
  184.0 10.2 %copy-start.14 = (bf16[384,2,512]{2,0,1:T(8,128)(2,1)}, bf16[384,2,512]{2,0,1:T(8,128)(2,1)S(1)}, u32[]{:S(2)}) copy-start(bf16[384,2,512]{2,0,1:T(8,128)(2,1)S(1)} %collective-permute-done.5) | copy-start | bytes 2359300
  184.0 5.5 %collective-permute-start.6 = (bf16[384,2,512]{2,0,1:T(8,128)(2,1)S(1)}, bf16[384,2,512]{2,0,1:T(8,128)(2,1)}, u32[]{:S(2)}, u32[]{:S(2)}) collective-permute-start(bf16[384,2,512]{2,0,1:T(8,128)(2,1)S(1)} %collective-permute-done.5), channel_id=1, source_target_pairs={{0,2},{2,4},{4,6},{6,8},{8,10},{10,12},{12,14},{14,16},{16,18},{18... | collective-permute-start | bytes 2359304 | tf_op jit(solution)/shard_map/ppermute | solution.py:19
  189.6 13.6 %collective-permute-start.7 = (bf16[384,2,512]{2,0,1:T(8,128)(2,1)}, bf16[384,2,512]{2,0,1:T(8,128)(2,1)}, u32[]{:S(2)}, u32[]{:S(2)}) collective-permute-start(bf16[384,2,512]{2,0,1:T(8,128)(2,1)} %collective-permute-done.6), channel_id=1, source_target_pairs={{0,2},{2,4},{4,6},{6,8},{8,10},{10,12},{12,14},{14,16},{16,18},{18... | collective-permute-start | bytes 2359304 | tf_op jit(solution)/shard_map/ppermute | solution.py:19
  194.1 18.3 %copy-start.13 = (bf16[384,2,512]{2,0,1:T(8,128)(2,1)S(1)}, bf16[384,2,512]{2,0,1:T(8,128)(2,1)}, u32[]{:S(2)}) copy-start(bf16[384,2,512]{2,0,1:T(8,128)(2,1)} %copy-done.12) | copy-start | bytes 2359300
  194.3 13.0 %copy-start.15 = (bf16[384,2,512]{2,0,1:T(8,128)(2,1)S(1)}, bf16[384,2,512]{2,0,1:T(8,128)(2,1)}, u32[]{:S(2)}) copy-start(bf16[384,2,512]{2,0,1:T(8,128)(2,1)} %copy-done.14) | copy-start | bytes 2359300
  194.3 19.1 %copy-start.11 = (bf16[384,2,512]{2,0,1:T(8,128)(2,1)S(1)}, bf16[384,2,512]{2,0,1:T(8,128)(2,1)}, u32[]{:S(2)}) copy-start(bf16[384,2,512]{2,0,1:T(8,128)(2,1)} %copy-done.10) | copy-start | bytes 2359300
  197.2 17.1 %copy-start.9 = (bf16[384,2,512]{2,0,1:T(8,128)(2,1)S(1)}, bf16[384,2,512]{2,0,1:T(8,128)(2,1)}, u32[]{:S(2)}) copy-start(bf16[384,2,512]{2,0,1:T(8,128)(2,1)} %copy-done.8) | copy-start | bytes 2359300
  197.2 18.1 %copy-start.5 = (bf16[384,512]{1,0:T(8,128)(2,1)S(1)}, bf16[384,512]{1,0:T(8,128)(2,1)}, u32[]{:S(2)}) copy-start(bf16[384,512]{1,0:T(8,128)(2,1)} %param.10) | copy-start | bytes 1179652
  197.2 18.1 %copy-start.6 = (bf16[384,512]{1,0:T(8,128)(2,1)S(1)}, bf16[384,512]{1,0:T(8,128)(2,1)}, u32[]{:S(2)}) copy-start(bf16[384,512]{1,0:T(8,128)(2,1)} %param.11) | copy-start | bytes 1179652
  237.2 13.4 %copy-start.3 = (bf16[6,64,2,4,128]{4,1,3,2,0:T(8,128)(2,1)}, bf16[6,64,2,4,128]{4,1,3,2,0:T(8,128)(2,1)S(1)}, u32[]{:S(2)}) copy-start(bf16[6,64,2,4,128]{4,1,3,2,0:T(8,128)(2,1)S(1)} %get-tuple-element.346) | copy-start | bytes 2359300 | tf_op jit(solution)/shard_map/while
  312.0 12.2 %copy-start.2 = (bf16[4,3,15,64,1,128]{5,3,4,2,1,0:T(8,128)(2,1)S(1)}, bf16[4,3,15,64,1,128]{5,3,4,2,1,0:T(8,128)(2,1)}, u32[]{:S(2)}) copy-start(bf16[4,3,15,64,1,128]{5,3,4,2,1,0:T(8,128)(2,1)} %get-tuple-element.309) | copy-start | bytes 8847364 | tf_op jit(solution)/shard_map/while
  324.2 13.2 %copy-start.4 = (bf16[6,64,2,4,128]{4,1,3,2,0:T(8,128)(2,1)S(1)}, bf16[6,64,2,4,128]{4,1,3,2,0:T(8,128)(2,1)}, u32[]{:S(2)}) copy-start(bf16[6,64,2,4,128]{4,1,3,2,0:T(8,128)(2,1)} %copy-done.3) | copy-start | bytes 2359300 | tf_op jit(solution)/shard_map/while
  337.4 13.4 %copy-start.3 = (bf16[6,64,2,4,128]{4,1,3,2,0:T(8,128)(2,1)}, bf16[6,64,2,4,128]{4,1,3,2,0:T(8,128)(2,1)S(1)}, u32[]{:S(2)}) copy-start(bf16[6,64,2,4,128]{4,1,3,2,0:T(8,128)(2,1)S(1)} %get-tuple-element.346) | copy-start | bytes 2359300 | tf_op jit(solution)/shard_map/while
  412.2 12.2 %copy-start.2 = (bf16[4,3,15,64,1,128]{5,3,4,2,1,0:T(8,128)(2,1)S(1)}, bf16[4,3,15,64,1,128]{5,3,4,2,1,0:T(8,128)(2,1)}, u32[]{:S(2)}) copy-start(bf16[4,3,15,64,1,128]{5,3,4,2,1,0:T(8,128)(2,1)} %get-tuple-element.309) | copy-start | bytes 8847364 | tf_op jit(solution)/shard_map/while
  424.4 13.2 %copy-start.4 = (bf16[6,64,2,4,128]{4,1,3,2,0:T(8,128)(2,1)S(1)}, bf16[6,64,2,4,128]{4,1,3,2,0:T(8,128)(2,1)}, u32[]{:S(2)}) copy-start(bf16[6,64,2,4,128]{4,1,3,2,0:T(8,128)(2,1)} %copy-done.3) | copy-start | bytes 2359300 | tf_op jit(solution)/shard_map/while
  440.5 66.3 %copy-start.1 = (s32[96]{0:T(128)S(1)}, s32[96]{0:T(128)}, u32[]{:S(2)}) copy-start(s32[96]{0:T(128)} %param.14) | copy-start | bytes 1156
Sparse Core Ops, SparseCore 0:
  452.1 54.5 reduce-scatter.1
where the time goes:
time: 517 us; the launch traced here: 514 us
  blocking collectives  114 us (22%)
  waiting for transfers between devices  109 us (21%)
  matrix products  102 us (20%)
  local copies, waits for them, and re-layouts  98.5 us (19%)
  other arithmetic  65.1 us (13%)
  between operations  13.7 us (3%)
  starting transfers between devices  10.3 us (2%)
    psum x1, blocking collectives, per_device(): columns = lax.psum(contrib, 'context').astype(jnp.bfloat16)  114 us
    reduce_scatter x1, waiting for transfers between devices, per_device(): lax.psum_scatter(jnp.dot(attended, out_weight, preferred_element_type=jnp...  54.8 us
    ppermute x8, waiting for transfers between devices, shifted(): lax.ppermute(value, axis, [(source, source + steps) for source in range(i...  54.3 us
    reduce_sum x2, other arithmetic, attend(): jnp.sum(weight_cols, axis=(-2, -1))  33.9 us
    gather x2, local copies, waits for them, and re-layouts, attend(): band = ext_blocks[band_pos, :, :, head_ids[:, :, None]]  30.3 us
    reduce_sum x2, other arithmetic, attend(): jnp.sum(weight_band, axis=(-2, -1))  24.4 us
    dot_general x2, matrix products, attend(): jnp.einsum('bghrnc,gbncd->brghd', weight_band.astype(jnp.bfloat16), band[...  23.3 us
    dot_general x2, matrix products, attend(): jnp.einsum('brghd,gncd->bghrnc', q_part, column_keys, preferred_element_t...  21.2 us
  transfers between devices with their start and end apart: 9, of which 8 were waited for; matrix products, arithmetic and copies ran while one was open for 3% of the time, Pallas kernels for 0%

commit v1 on v0

v1 whole, which is shorter than its diff:
```python
import functools

import jax
import jax.numpy as jnp
from jax import lax
from jax.experimental import pallas as pl
from jax.experimental.pallas import tpu as pltpu
from jax.sharding import PartitionSpec as P

QH = 32
KVH = 8
HD = 128
BLOCK = 64
GROUP = QH // KVH
SPAN = 8
WIDE = SPAN * BLOCK

floor_score = -1e30
exp2_scale = HD ** (-0.5) * 1.4426950408889634


def plan(vert_cols, slash_off, doc_ids, context, blocks):
    query_block = context * blocks + jnp.arange(blocks, dtype=jnp.int32)
    query_doc = lax.dynamic_slice_in_dim(doc_ids, context * blocks, blocks, 0)
    doc_start = jnp.sum((doc_ids[None, :] < query_doc[:, None]).astype(jnp.int32), axis=1)
    at = query_block[None, :, None]
    start = doc_start[None, :, None]
    slash_key = at - slash_off[:, None, :]
    slash_live = slash_key >= start
    column = jnp.broadcast_to(
        (vert_cols // BLOCK)[:, None, :], (vert_cols.shape[0], blocks, vert_cols.shape[1])
    )
    on_slash = jnp.any((at - column)[..., None] == slash_off[:, None, None, :], axis=-1)
    column_live = (column < at) & jnp.logical_not(on_slash & (column >= start))
    diagonal = jnp.broadcast_to(at, slash_key.shape[:2] + (1,))
    ids = jnp.concatenate([diagonal, slash_key, column], axis=-1)
    live = jnp.concatenate([diagonal >= 0, slash_live, column_live], axis=-1)
    seats = -(-ids.shape[-1] // SPAN) * SPAN
    order = jnp.arange(ids.shape[-1])
    seat = jnp.sum(
        (live[..., None, :] & (order[None, :] < order[:, None])).astype(jnp.int32), axis=-1
    )
    count = jnp.sum(live.astype(jnp.int32), axis=-1)
    chosen = live[..., None, :] & (seat[..., None, :] == jnp.arange(seats)[:, None])
    packed = jnp.sum(jnp.where(chosen, ids[..., None, :], 0), axis=-1)
    packed = jnp.where(jnp.arange(seats) < count[..., None], packed, at)
    return packed.reshape(-1), count.reshape(-1), seats


def attend_kernel(blocks, seats, ids_ref, count_ref, q_ref, k_ref, v_ref, o_ref, s_ref):
    head = pl.program_id(0)

    def one(index, carry):
        pair = head * blocks + index
        count = count_ref[pair]
        chunks = (count + SPAN - 1) // SPAN
        rows = pl.ds(pl.multiple_of(index * BLOCK, BLOCK), BLOCK)
        q = jnp.concatenate([q_ref[rows, g * HD:(g + 1) * HD] for g in range(GROUP)], axis=0)

        def gathered(ref, chunk):
            parts = []
            for j in range(SPAN):
                where = ids_ref[pair * seats + chunk * SPAN + j]
                parts.append(ref[pl.ds(pl.multiple_of(where * BLOCK, BLOCK), BLOCK), :])
            return jnp.concatenate(parts, axis=0)

        def whole(number):
            most = None
            for chunk in range(number):
                s = lax.dot_general(
                    q, gathered(k_ref, chunk), (((1,), (1,)), ((), ())),
                    preferred_element_type=jnp.float32,
                )
                lane = lax.broadcasted_iota(jnp.int32, s.shape, 1)
                if chunk == 0:
                    row = lax.broadcasted_iota(jnp.int32, s.shape, 0) % BLOCK
                    s = jnp.where((lane > row) & (lane < BLOCK), floor_score, s)
                if chunk == number - 1:
                    s = jnp.where(lane < (count - chunk * SPAN) * BLOCK, s, floor_score)
                s_ref[:, chunk * WIDE:(chunk + 1) * WIDE] = s
                for part in range(0, WIDE, HD):
                    piece = s[:, part:part + HD]
                    most = piece if most is None else jnp.maximum(most, piece)
            top = jnp.max(most, axis=1, keepdims=True)
            summed = None
            total = None
            for chunk in range(number):
                s = s_ref[:, chunk * WIDE:(chunk + 1) * WIDE]
                p = jnp.exp2((s - top) * exp2_scale)
                for part in range(0, WIDE, HD):
                    piece = p[:, part:part + HD]
                    total = piece if total is None else total + piece
                out = jnp.dot(
                    p.astype(jnp.bfloat16), gathered(v_ref, chunk),
                    preferred_element_type=jnp.float32,
                )
                summed = out if summed is None else summed + out
            out = (summed / jnp.sum(total, axis=1, keepdims=True)).astype(jnp.bfloat16)
            for g in range(GROUP):
                o_ref[rows, g * HD:(g + 1) * HD] = out[g * BLOCK:(g + 1) * BLOCK]

        for number in range(1, seats // SPAN + 1):
            pl.when(chunks == number)(functools.partial(whole, number))
        return carry

    lax.fori_loop(0, blocks, one, 0)


def attend(query, keys, values, ids, count, seats):
    rows = query.shape[0]
    heads = keys.shape[1] // HD
    blocks = rows // BLOCK
    tokens = keys.shape[0]
    return pl.pallas_call(
        functools.partial(attend_kernel, blocks, seats),
        grid=(heads,),
        out_shape=jax.ShapeDtypeStruct(query.shape, jnp.bfloat16),
        in_specs=[
            pl.BlockSpec(memory_space=pltpu.SMEM),
            pl.BlockSpec(memory_space=pltpu.SMEM),
            pl.BlockSpec((rows, GROUP * HD), lambda h: (0, h)),
            pl.BlockSpec((tokens, HD), lambda h: (0, h)),
            pl.BlockSpec((tokens, HD), lambda h: (0, h)),
        ],
        out_specs=pl.BlockSpec((rows, GROUP * HD), lambda h: (0, h)),
        scratch_shapes=[pltpu.VMEM((GROUP * BLOCK, seats * BLOCK), jnp.float32)],
        compiler_params=pltpu.CompilerParams(vmem_limit_bytes=48 * 1024 * 1024),
        name="attend",
    )(ids, count, query, keys, values)


def per_device(query, keys, values, vert_cols, slash_off, doc_ids, out_weight):
    blocks = keys.shape[0] // BLOCK
    context = lax.axis_index("context")
    ids, count, seats = plan(vert_cols, slash_off, doc_ids, context, blocks)
    all_keys = lax.all_gather(keys, "context", axis=0, tiled=True)
    all_values = lax.all_gather(values, "context", axis=0, tiled=True)
    attended = attend(query, all_keys, all_values, ids, count, seats)
    return lax.psum_scatter(
        jnp.dot(attended, out_weight, preferred_element_type=jnp.float32).astype(jnp.bfloat16),
        "tensor",
        scatter_dimension=0,
        tiled=True,
    )


def solution(mesh):
    placed = (
        P("context", "tensor"),
        P("context", "tensor"),
        P("context", "tensor"),
        P("tensor", None),
        P("tensor", None),
        P(),
        P("tensor", None),
    )
    return jax.shard_map(
        per_device,
        mesh=mesh,
        in_specs=placed,
        out_specs=P(("context", "tensor"), None),
        check_vma=False,
    )
```

time: 517 us -> 226 us (0.44)
  blocking collectives: 114 us -> 0 us
  local copies, waits for them, and re-layouts: 98.5 us -> 3.32 us
  matrix products: 102 us -> 11.4 us
  other arithmetic: 65.1 us -> 4.73 us
  waiting for transfers between devices: 109 us -> 169 us
  Pallas kernels: 0 us -> 22.1 us
  starting transfers between devices: 10.3 us -> 0.08 us
    all_gather x0 -> x2, waiting for transfers between devices: none -> 119 us  [the longest x1 62.8 us: per_device(): all_values = lax.all_gather(values, 'context', axis=0, tiled=True)]
    psum x1 -> x0, blocking collectives: 114 us -> none  [per_device(): columns = lax.psum(contrib, 'context').astype(jnp.bfloat16)]
    dot_general x12 -> x0, matrix products: 90.3 us -> none  [the longest x2 23.3 us: attend(): jnp.einsum('bghrnc,gbncd->brghd', weight_band.astype(jnp.bfloat16), band[...]
    reduce_sum x6 -> x4, other arithmetic: 59.1 us -> 2.05 us  [the longest x1 0.84 us: plan(): jnp.sum((doc_ids[None, :] < query_doc[:, None]).astype(jnp.int32), axis=1)]
    ppermute x8 -> x0, waiting for transfers between devices: 54.3 us -> none  [shifted(): lax.ppermute(value, axis, [(source, source + steps) for source in range(i...]
    gather x8 -> x0, local copies, waits for them, and re-layouts: 35.6 us -> none  [the longest x2 30.3 us: attend(): band = ext_blocks[band_pos, :, :, head_ids[:, :, None]]]
    pallas_call x0 -> x1, Pallas kernels: none -> 22.1 us  [attend(): pl.pallas_call(functools.partial(attend_kernel, blocks, seats), grid=(hea...]
    unnamed x40 -> x3, local copies, waits for them, and re-layouts: 20.4 us -> 2.18 us
  transfers between devices with their start and end apart: 9 -> 3, of which waited for: 8 -> 3; matrix products, arithmetic and copies ran while one was open for 3% -> 3% of each run, Pallas kernels for 0% -> 0%
where the time goes in v1:
time: 226 us; the launch traced here: 223 us
  waiting for transfers between devices  169 us (75%)
  Pallas kernels  22.1 us (10%)
  between operations  13.2 us (6%)
  matrix products  11.4 us (5%)
  other arithmetic  4.73 us (2%)
  local copies, waits for them, and re-layouts  3.32 us (1%)
    all_gather x1, waiting for transfers between devices, per_device(): all_values = lax.all_gather(values, 'context', axis=0, tiled=True)  62.8 us
    all_gather x1, waiting for transfers between devices, per_device(): all_keys = lax.all_gather(keys, 'context', axis=0, tiled=True)  55.9 us
    reduce_scatter x1, waiting for transfers between devices, per_device(): lax.psum_scatter(jnp.dot(attended, out_weight, preferred_element_type=jnp...  48.5 us
    pallas_call x1, Pallas kernels, attend(): pl.pallas_call(functools.partial(attend_kernel, blocks, seats), grid=(hea...  22.1 us
    dot_general x1, matrix products, per_device(): jnp.dot(attended, out_weight, preferred_element_type=jnp.float32)  11.4 us
  transfers between devices with their start and end apart: 3, of which 3 were waited for; matrix products, arithmetic and copies ran while one was open for 3% of the time, Pallas kernels for 0%

profile of v1, /device:TPU:27, one launch (start us, length us, event | category | flops | bytes accessed | tf_op | source)
XLA Modules:
  0.0 223.4 jit_solution(2668863678313464220)
XLA Ops:
  6.5 0.0 all-gather.3.cloned.1.call-start
  6.5 0.7 all-gather.3.cloned.1.call-update
  7.3 0.0 all-gather.5.cloned.1.call-start
  7.3 0.7 all-gather.5.cloned.1.call-update
  8.0 0.0 reduce-scatter.2.cloned.1.call-start
  8.1 0.8 copy.8
  8.8 0.7 dynamic_slice.3
  9.6 0.8 convert_reduce_fusion.2
  10.4 0.7 add_select_fusion
  11.1 0.1 broadcast_subtract_fusion
  11.2 0.1 compare_reduce_fusion
  11.3 0.8 broadcast_compare_fusion
  12.1 0.1 not_and_fusion
  12.2 0.1 broadcast_in_dim.19
  12.2 0.2 convert_reduce_fusion.1
  12.5 0.1 copy.9
  12.6 0.1 reshape.46.count_ref
  12.7 0.8 broadcast_subtract_fusion.1
  13.4 0.1 broadcast_in_dim.21
  13.5 0.1 pad_add_fusion
  13.6 0.5 convert_reduce_fusion
  14.1 0.5 select_reduce_fusion
  14.6 0.1 fusion.1
  14.7 0.1 select_n.24.ids_ref
  14.8 55.9 %all-gather.3.cloned.1.call-done.k_ref = bf16[6144,512]{1,0:T(8,128)(2,1)} async-done(((bf16[384,512]{1,0:T(8,128)(2,1)}), bf16[6144,512]{1,0:T(8,128)(2,1)}) %all-gather.3.cloned.1.call-update) | async-done | bytes 6291472 | tf_op jit(solution)/shard_map/all_gather | solution.py:136
  70.6 62.8 %all-gather.5.cloned.1.call-done.v_ref = bf16[6144,512]{1,0:T(8,128)(2,1)} async-done(((bf16[384,512]{1,0:T(8,128)(2,1)}), bf16[6144,512]{1,0:T(8,128)(2,1)}) %all-gather.5.cloned.1.call-update) | async-done | bytes 6291472 | tf_op jit(solution)/shard_map/all_gather | solution.py:137
  133.4 0.0 copy-start
  133.4 1.4 copy-done
  134.8 22.1 %attend.1 = bf16[384,2048]{1,0:T(8,128)(2,1)S(1)} custom-call(s32[768]{0:T(1024)S(1)} %select_n.24.ids_ref, s32[24]{0:T(128)S(1)} %reshape.46.count_ref, bf16[384,2048]{1,0:T(8,128)(2,1)S(1)} %copy-done, bf16[6144,512]{1,0:T(8,128)(2,1)} %all-gather.3.cloned.1.call-done.k_ref, bf16[6144,512]{1,0:T(8,128)(2,1)} %all-gather.5.cloned.1.call-done.v_ref), custom_call_target="tpu_custom_call" | custom-call | tf_op jit(solution)/shard_map/attend/pallas_call | solution.py:114
  156.9 11.4 %convolution_convert_fusion = bf16[384,4096]{1,0:T(8,128)(2,1)} fusion(bf16[384,2048]{1,0:T(8,128)(2,1)S(1)} %attend.1, bf16[2048,4096]{1,0:T(8,128)(2,1)} %param.13), kind=kOutput, calls=%fused_computation | convolution fusion | flops 6444023808 | bytes 21495808 | tf_op jit(solution)/shard_map/dot_general | solution.py:140
  168.3 0.0 reduce-scatter.2.cloned.1.call-update
  168.3 48.5 %reduce-scatter.2.cloned.1.call-done = bf16[192,4096]{1,0:T(8,128)(2,1)} async-done(((bf16[384,4096]{1,0:T(8,128)(2,1)}), bf16[192,4096]{1,0:T(8,128)(2,1)}) %reduce-scatter.2.cloned.1.call-update) | async-done | bytes 1572880 | tf_op jit(solution)/shard_map/reduce_scatter | solution.py:139
  (6 shorter events, 0.0 us)
Async XLA Ops:
  6.5 64.1 %all-gather.3.cloned.1.call-start = ((), (), s32[]{:S(2)}) async-start(), calls=%async_computation.1 | async-start | bytes 6684672 | tf_op jit(solution)/shard_map/all_gather | solution.py:136
  7.3 126.1 %all-gather.5.cloned.1.call-start = ((), (), s32[]{:S(2)}) async-start(), calls=%async_computation.2 | async-start | bytes 6684672 | tf_op jit(solution)/shard_map/all_gather | solution.py:137
  8.0 208.8 %reduce-scatter.2.cloned.1.call-start = ((), (), s32[]{:S(2)}) async-start(), calls=%async_computation.3 | async-start | bytes 4718592 | tf_op jit(solution)/shard_map/reduce_scatter | solution.py:139
  133.4 1.4 copy-start
Sparse Core Ops, SparseCore 0:
  9.6 60.9 all-gather.2
  72.9 60.4 all-gather.4
  168.5 48.3 reduce-scatter.1

commit v2 on v1

--- a/solution.py
+++ b/solution.py
@@ -47,11 +47,12 @@
     return packed.reshape(-1), count.reshape(-1), seats
 
 
-def attend_kernel(blocks, seats, ids_ref, count_ref, q_ref, k_ref, v_ref, o_ref, s_ref):
+def attend_kernel(blocks, here, seats, part_ref, ids_ref, count_ref, q_ref, k_ref, v_ref, o_ref, s_ref):
     head = pl.program_id(0)
+    lead = part_ref[0] * here
 
     def one(index, carry):
-        pair = head * blocks + index
+        pair = head * blocks + lead + index
         count = count_ref[pair]
         chunks = (count + SPAN - 1) // SPAN
         rows = pl.ds(pl.multiple_of(index * BLOCK, BLOCK), BLOCK)
@@ -103,45 +104,187 @@
             pl.when(chunks == number)(functools.partial(whole, number))
         return carry
 
-    lax.fori_loop(0, blocks, one, 0)
-
-
-def attend(query, keys, values, ids, count, seats):
-    rows = query.shape[0]
+    lax.fori_loop(0, here, one, 0)
+
+
+def attend(query, keys, values, part, parts, ids, count, seats):
+    rows = query.shape[0] // parts
     heads = keys.shape[1] // HD
-    blocks = rows // BLOCK
     tokens = keys.shape[0]
+    grid_spec = pltpu.PrefetchScalarGridSpec(
+        num_scalar_prefetch=3,
+        grid=(heads,),
+        in_specs=[
+            pl.BlockSpec((rows, GROUP * HD), lambda h, part_ref, *_: (part_ref[0], h)),
+            pl.BlockSpec((tokens, HD), lambda h, *_: (0, h)),
+            pl.BlockSpec((tokens, HD), lambda h, *_: (0, h)),
+        ],
+        out_specs=pl.BlockSpec((rows, GROUP * HD), lambda h, *_: (0, h)),
+        scratch_shapes=[pltpu.VMEM((GROUP * BLOCK, seats * BLOCK), jnp.float32)],
+    )
+    pairs = heads * rows * GROUP
     return pl.pallas_call(
-        functools.partial(attend_kernel, blocks, seats),
-        grid=(heads,),
-        out_shape=jax.ShapeDtypeStruct(query.shape, jnp.bfloat16),
-        in_specs=[
-            pl.BlockSpec(memory_space=pltpu.SMEM),
-            pl.BlockSpec(memory_space=pltpu.SMEM),
-            pl.BlockSpec((rows, GROUP * HD), lambda h: (0, h)),
-            pl.BlockSpec((tokens, HD), lambda h: (0, h)),
-            pl.BlockSpec((tokens, HD), lambda h: (0, h)),
+        functools.partial(attend_kernel, query.shape[0] // BLOCK, rows // BLOCK, seats),
+        grid_spec=grid_spec,
+        out_shape=jax.ShapeDtypeStruct((rows, query.shape[1]), jnp.bfloat16),
+        compiler_params=pltpu.CompilerParams(vmem_limit_bytes=48 * 1024 * 1024),
+        cost_estimate=pl.CostEstimate(
+            flops=4 * pairs * seats * BLOCK * HD,
+            bytes_accessed=4 * tokens * heads * HD,
+            transcendentals=pairs * seats * BLOCK,
+        ),
+        name="attend",
+    )(part.reshape(1), ids, count, query, keys, values)
+
+
+LEVEL = 4
+
+
+def gather_kernel(levels, k_ref, v_ref, gk_ref, gv_ref, send_sem, recv_sem, own_sem):
+    rows = k_ref.shape[0]
+    me = lax.axis_index("context")
+    level = me // LEVEL
+    side = (me // 2) % 2
+    core = me % 2
+    over = me + 2 - 4 * side
+    twin = me + 1 - 2 * core
+    last = level == levels - 1
+
+    barrier = pltpu.get_barrier_semaphore()
+
+    def greet(device):
+        pl.semaphore_signal(
+            barrier, inc=1, device_id={"context": device}, device_id_type=pl.DeviceIdType.MESH
+        )
+
+    greet(over)
+    greet(twin)
+    pl.when(level > 0)(lambda: greet(me - LEVEL))
+    pl.when(level < levels - 1)(lambda: greet(me + LEVEL))
+    pl.semaphore_wait(
+        barrier, 2 + jnp.where(level > 0, 1, 0) + jnp.where(level < levels - 1, 1, 0)
+    )
+
+    inputs, gathered = (k_ref, v_ref), (gk_ref, gv_ref)
+
+    def place(owner, part):
+        return gathered[part].at[pl.ds(pl.multiple_of(owner * rows, rows), rows), :]
+
+    def copy(owner, part, device, sem, own=False):
+        return pltpu.make_async_remote_copy(
+            src_ref=inputs[part] if own else place(owner, part),
+            dst_ref=place(owner, part),
+            send_sem=send_sem.at[sem],
+            recv_sem=recv_sem.at[owner, part],
+            device_id={"context": device},
+            device_id_type=pl.DeviceIdType.MESH,
+        )
+
+    def sem_of(kind, step, part):
+        return (kind * levels + step) * 2 + part
+
+    sent = []
+
+    def send(condition, *args, **kwargs):
+        pl.when(condition)(lambda: copy(*args, **kwargs).start())
+        sent.append((condition, args, kwargs))
+
+    def arrive(condition, owner, part):
+        pl.when(condition)(lambda: copy(owner, part, twin, 0).wait_recv())
+
+    own_copies = [
+        pltpu.make_async_copy(inputs[part], place(me, part), own_sem.at[part]) for part in range(2)
+    ]
+    for own_copy in own_copies:
+        own_copy.start()
+
+    climber = core
+    for step in range(levels + 1):
+        from_level = level - step
+        if step < levels:
+            held = from_level >= 0
+            owner = from_level * LEVEL + side * 2 + core
+            for part in range(2):
+                if step:
+                    arrive(held, owner, part)
+                send(held & (level < levels - 1), owner, part, me + LEVEL, sem_of(0, step, part), own=step == 0)
+                crosses = held & (side == 0) if step == 0 else held
+                if part == 0 and step > 0:
+                    crosses = crosses & jnp.logical_not((from_level == 0) & (side == 0))
+                send(crosses, owner, part, over, sem_of(1, step, part), own=step == 0)
+                send(held & (core == 0) if step == 0 else held, owner, part, twin, sem_of(2, step, part), own=step == 0)
+        if step:
+            back = step - 1
+            before = level - back
+            owner = before * LEVEL + (1 - side) * 2 + core
+            for part in range(2):
+                crossed = (before >= 0) & (side == 1) if back == 0 else before >= 0
+                arrive(crossed, owner, part)
+                if part == 0:
+                    climbs = crossed & (before == 0) & (side == 1)
+                    send(climbs & (level < levels - 1), owner, part, me + LEVEL, sem_of(4, back, part))
+                send(crossed, owner, part, twin, sem_of(3, back, part))
+    for before in range(levels):
+        for other in range(2):
+            for part in range(2):
+                owner = before * LEVEL + other * 2 + 1 - core
+                mine = (before == level) & ((other < side) | ((other == side) & (core == 1)))
+                arrive((before < level) | mine, owner, part)
+    for condition, args, kwargs in sent:
+        pl.when(condition)(lambda args=args, kwargs=kwargs: copy(*args, **kwargs).wait_send())
+    for own_copy in own_copies:
+        own_copy.wait()
+
+
+def gather(keys, values, count):
+    levels = count // LEVEL
+    shape = jax.ShapeDtypeStruct((count * keys.shape[0], keys.shape[1]), keys.dtype)
+    return pl.pallas_call(
+        functools.partial(gather_kernel, levels),
+        out_shape=(shape, shape),
+        in_specs=[pl.BlockSpec(memory_space=pl.ANY)] * 2,
+        out_specs=(pl.BlockSpec(memory_space=pl.ANY),) * 2,
+        scratch_shapes=[
+            pltpu.SemaphoreType.DMA((5 * levels * 2,)),
+            pltpu.SemaphoreType.DMA((count, 2)),
+            pltpu.SemaphoreType.DMA((2,)),
         ],
-        out_specs=pl.BlockSpec((rows, GROUP * HD), lambda h: (0, h)),
-        scratch_shapes=[pltpu.VMEM((GROUP * BLOCK, seats * BLOCK), jnp.float32)],
-        compiler_params=pltpu.CompilerParams(vmem_limit_bytes=48 * 1024 * 1024),
-        name="attend",
-    )(ids, count, query, keys, values)
+        compiler_params=pltpu.CompilerParams(collective_id=0, has_side_effects=True),
+        name="gather",
+    )(keys, values)
 
 
 def per_device(query, keys, values, vert_cols, slash_off, doc_ids, out_weight):
     blocks = keys.shape[0] // BLOCK
     context = lax.axis_index("context")
+    tensor = lax.axis_index("tensor")
+    shares = lax.axis_size("tensor")
     ids, count, seats = plan(vert_cols, slash_off, doc_ids, context, blocks)
-    all_keys = lax.all_gather(keys, "context", axis=0, tiled=True)
-    all_values = lax.all_gather(values, "context", axis=0, tiled=True)
-    attended = attend(query, all_keys, all_values, ids, count, seats)
-    return lax.psum_scatter(
-        jnp.dot(attended, out_weight, preferred_element_type=jnp.float32).astype(jnp.bfloat16),
-        "tensor",
-        scatter_dimension=0,
-        tiled=True,
-    )
+    all_keys, all_values = gather(keys, values, lax.axis_size("context"))
+
+    def projected(rows, weight):
+        return jnp.dot(rows, weight, preferred_element_type=jnp.float32).astype(jnp.bfloat16)
+
+    if shares != 2 or blocks % shares:
+        first = jnp.zeros((), jnp.int32)
+        rows = attend(query, all_keys, all_values, first, 1, ids, count, seats)
+        return lax.psum_scatter(
+            projected(rows, out_weight), "tensor", scatter_dimension=0, tiled=True
+        )
+    theirs = attend(query, all_keys, all_values, 1 - tensor, shares, ids, count, seats)
+    cuts = 2
+    width = out_weight.shape[1] // cuts
+    moved = []
+    for cut in range(cuts):
+        weight = out_weight[:, cut * width:(cut + 1) * width]
+        moved.append(lax.ppermute(projected(theirs, weight), "tensor", [(0, 1), (1, 0)]))
+    part, _ = lax.optimization_barrier((tensor, theirs))
+    mine = attend(query, all_keys, all_values, part, shares, ids, count, seats)
+    outs = []
+    for cut in range(cuts):
+        weight = out_weight[:, cut * width:(cut + 1) * width]
+        outs.append(projected(mine, weight).astype(jnp.float32) + moved[cut].astype(jnp.float32))
+    return jnp.concatenate(outs, axis=1).astype(jnp.bfloat16)
 
 
 def solution(mesh):

time: 226 us -> 137 us (0.61)
  waiting for transfers between devices: 169 us -> 10.1 us
  Pallas kernels: 22.1 us -> 93.4 us
  between operations: 13.2 us -> 0.14 us
  matrix products: 11.4 us -> 20.8 us
    all_gather x2 -> x0, waiting for transfers between devices: 119 us -> none  [the longest x1 62.8 us: per_device(): all_values = lax.all_gather(values, 'context', axis=0, tiled=True)]
    pallas_call x1 -> x3, Pallas kernels: 22.1 us -> 93.4 us  [the longest x1 65.4 us: gather(): pl.pallas_call(functools.partial(gather_kernel, levels), out_shape=(shape...]
    reduce_scatter x1 -> x0, waiting for transfers between devices: 48.5 us -> none  [per_device(): lax.psum_scatter(jnp.dot(attended, out_weight, preferred_element_type=jnp...]
    ppermute x0 -> x2, waiting for transfers between devices: none -> 10.1 us  [per_device(): lax.ppermute(projected(theirs, weight), 'tensor', [(0, 1), (1, 0)])]
    dot_general x1 -> x4, matrix products: 11.4 us -> 20.8 us  [projected(): jnp.dot(rows, weight, preferred_element_type=jnp.float32)]
  transfers between devices with their start and end apart: 3 -> 2, of which waited for: 3 -> 1; matrix products, arithmetic and copies ran while one was open for 3% -> 8% of each run, Pallas kernels for 0% -> 10%
where the time goes in v2:
time: 137 us; the launch traced here: 135 us
  Pallas kernels  93.4 us (68%)
  matrix products  20.8 us (15%)
  waiting for transfers between devices  10.1 us (7%)
  other arithmetic  6.01 us (4%)
  local copies, waits for them, and re-layouts  3.33 us (2%)
  starting transfers between devices  1.56 us (1%)
    pallas_call x1, Pallas kernels, gather(): pl.pallas_call(functools.partial(gather_kernel, levels), out_shape=(shape...  65.4 us
    pallas_call x2, Pallas kernels, attend(): pl.pallas_call(functools.partial(attend_kernel, query.shape[0] // BLOCK,...  28.1 us
    dot_general x4, matrix products, projected(): jnp.dot(rows, weight, preferred_element_type=jnp.float32)  20.8 us
    ppermute x2, waiting for transfers between devices, per_device(): lax.ppermute(projected(theirs, weight), 'tensor', [(0, 1), (1, 0)])  10.1 us
  transfers between devices with their start and end apart: 2, of which 1 were waited for; matrix products, arithmetic and copies ran while one was open for 8% of the time, Pallas kernels for 10%

profile of v2, /device:TPU:27, one launch (start us, length us, event | category | flops | bytes accessed | tf_op | source)
XLA Modules:
  0.0 135.4 jit_solution(8077847966695225198)
XLA Ops:
  0.0 0.7 dynamic_slice.3
  0.8 0.8 convert_reduce_fusion.2
  1.6 0.7 add_select_fusion
  2.3 0.8 copy.8
  3.1 0.8 broadcast_subtract_fusion.1
  3.8 0.8 broadcast_compare_fusion
  4.6 0.1 broadcast_subtract_fusion
  4.6 0.1 compare_reduce_fusion
  4.8 0.1 not_and_fusion
  4.9 0.1 broadcast_in_dim.19
  5.0 0.2 convert_reduce_fusion.1
  5.2 0.1 copy.9
  5.3 0.1 reshape.53.count_ref
  5.4 0.1 broadcast_in_dim.21
  5.5 0.1 pad_add_fusion
  5.6 0.5 convert_reduce_fusion
  6.1 0.5 select_reduce_fusion
  6.5 0.1 fusion.27
  6.6 0.1 select_n.24.ids_ref
  6.7 65.4 %gather.1 = (bf16[6144,512]{1,0:T(8,128)(2,1)}, bf16[6144,512]{1,0:T(8,128)(2,1)}) custom-call(bf16[384,512]{1,0:T(8,128)(2,1)} %k_ref.1, bf16[384,512]{1,0:T(8,128)(2,1)} %v_ref.1), custom_call_target="tpu_custom_call" | custom-call | tf_op jit(solution)/shard_map/gather/pallas_call | solution.py:242
  72.1 0.0 copy-start
  72.1 1.4 %copy-done = bf16[384,2048]{1,0:T(8,128)(2,1)S(1)} copy-done((bf16[384,2048]{1,0:T(8,128)(2,1)S(1)}, bf16[384,2048]{1,0:T(8,128)(2,1)}, u32[]{:S(2)}) %copy-start) | copy-done | bytes 1572888
  73.5 14.6 %attend.2 = bf16[192,2048]{1,0:T(8,128)(2,1)S(1)} custom-call(s32[1]{0:T(128)} %bitcast.part_ref, s32[768]{0:T(1024)S(1)} %select_n.24.ids_ref, s32[24]{0:T(128)S(1)} %reshape.53.count_ref, bf16[384,2048]{1,0:T(8,128)(2,1)S(1)} %copy-done, bf16[6144,512]{1,0:T(8,128)(2,1)} %get-tuple-element.8.k_ref, bf16[6144,512]{1,0:T(8,128)(2,1)} %get-tuple-element.9.v_ref), custom_call_target="tpu_custom_call" | custom-call | flops 3221225472 | bytes 12582912 | tf_op jit(solution)/shard_map/attend/pallas_call | solution.py:126
  88.1 5.2 %fusion.14 = bf16[192,2048]{1,0:T(8,128)(2,1)S(1)} fusion(bf16[192,2048]{1,0:T(8,128)(2,1)S(1)} %attend.2, bf16[2048,4096]{1,0:T(8,128)(2,1)} %param.13), kind=kOutput, calls=%fused_computation.10 | convolution fusion | flops 1611005952 | bytes 9961472 | tf_op jit(solution)/shard_map/dot_general | solution.py:266
  93.3 0.0 copy-start.1
  93.3 0.4 collective-permute-start
  93.7 5.2 %fusion.23 = bf16[192,2048]{1,0:T(8,128)(2,1)S(1)} fusion(bf16[192,2048]{1,0:T(8,128)(2,1)S(1)} %attend.2, bf16[2048,4096]{1,0:T(8,128)(2,1)} %param.13), kind=kOutput, calls=%fused_computation.13 | convolution fusion | flops 1611005952 | bytes 9961472 | tf_op jit(solution)/shard_map/dot_general | solution.py:266
  98.9 1.1 collective-permute-start.1
  100.1 0.0 copy-done.1
  100.1 13.5 %attend.3 = bf16[192,2048]{1,0:T(8,128)(2,1)S(1)} custom-call(s32[1]{0:T(128)} %bitcast.1.part_ref, s32[768]{0:T(1024)S(1)} %select_n.24.ids_ref, s32[24]{0:T(128)S(1)} %reshape.53.count_ref, bf16[384,2048]{1,0:T(8,128)(2,1)S(1)} %copy-done.1, bf16[6144,512]{1,0:T(8,128)(2,1)} %get-tuple-element.8.k_ref, bf16[6144,512]{1,0:T(8,128)(2,1)} %get-tuple-element.9.v_ref), custom_call_target="tpu_custom_call" | custom-call | flops 3221225472 | bytes 12582912 | tf_op jit(solution)/shard_map/attend/pallas_call | solution.py:126
  113.6 0.0 collective-permute-done
  113.6 5.2 %add_convert_fusion.1 = bf16[192,2048]{1,0:T(8,128)(2,1)S(1)} fusion(bf16[192,2048]{1,0:T(8,128)(2,1)S(1)} %collective-permute-done, bf16[192,2048]{1,0:T(8,128)(2,1)S(1)} %attend.3, bf16[2048,4096]{1,0:T(8,128)(2,1)} %param.13), kind=kOutput, calls=%fused_computation.16 | convolution fusion | flops 1612578816 | bytes 10747904 | tf_op jit(solution)/shard_map/dot_general | solution.py:266
  118.8 10.1 %collective-permute-done.1 = bf16[192,2048]{1,0:T(8,128)(2,1)S(1)} collective-permute-done((bf16[192,2048]{1,0:T(8,128)(2,1)S(1)}, bf16[192,2048]{1,0:T(8,128)(2,1)S(1)}, u32[]{:S(2)}, u32[]{:S(2)}) %collective-permute-start.1) | collective-permute-done | bytes 786464 | tf_op jit(solution)/shard_map/ppermute | solution.py:280
  128.9 5.2 %add_convert_fusion = bf16[192,2048]{1,0:T(8,128)(2,1)S(1)} fusion(bf16[192,2048]{1,0:T(8,128)(2,1)S(1)} %collective-permute-done.1, bf16[192,2048]{1,0:T(8,128)(2,1)S(1)} %attend.3, bf16[2048,4096]{1,0:T(8,128)(2,1)} %param.13), kind=kOutput, calls=%fused_computation.15 | convolution fusion | flops 1612578816 | bytes 10747904 | tf_op jit(solution)/shard_map/dot_general | solution.py:266
  134.1 1.3 pad_maximum_fusion
  (6 shorter events, 0.0 us)
Async XLA Ops:
  72.1 1.4 %copy-start = (bf16[384,2048]{1,0:T(8,128)(2,1)S(1)}, bf16[384,2048]{1,0:T(8,128)(2,1)}, u32[]{:S(2)}) copy-start(bf16[384,2048]{1,0:T(8,128)(2,1)} %q_ref.3) | copy-start | bytes 4718596
  93.3 6.8 %copy-start.1 = (bf16[384,2048]{1,0:T(8,128)(2,1)S(1)}, bf16[384,2048]{1,0:T(8,128)(2,1)}, u32[]{:S(2)}) copy-start(bf16[384,2048]{1,0:T(8,128)(2,1)} %q_ref.3) | copy-start | bytes 4718596
  93.3 20.3 %collective-permute-start = (bf16[192,2048]{1,0:T(8,128)(2,1)S(1)}, bf16[192,2048]{1,0:T(8,128)(2,1)S(1)}, u32[]{:S(2)}, u32[]{:S(2)}) collective-permute-start(bf16[192,2048]{1,0:T(8,128)(2,1)S(1)} %fusion.14), channel_id=1, source_target_pairs={{0,1},{1,0},{2,3},{3,2},{4,5},{5,4},{6,7},{7,6},{8,9},{9,8},{10,11... | collective-permute-start | bytes 2359304 | tf_op jit(solution)/shard_map/ppermute | solution.py:280
  98.9 30.0 %collective-permute-start.1 = (bf16[192,2048]{1,0:T(8,128)(2,1)S(1)}, bf16[192,2048]{1,0:T(8,128)(2,1)S(1)}, u32[]{:S(2)}, u32[]{:S(2)}) collective-permute-start(bf16[192,2048]{1,0:T(8,128)(2,1)S(1)} %fusion.23), channel_id=1, source_target_pairs={{0,1},{1,0},{2,3},{3,2},{4,5},{5,4},{6,7},{7,6},{8,9},{9,8},{10,11... | collective-permute-start | bytes 2359304 | tf_op jit(solution)/shard_map/ppermute | solution.py:280

commit v3 on v2

--- a/solution.py
+++ b/solution.py
@@ -135,6 +135,36 @@
         ),
         name="attend",
     )(part.reshape(1), ids, count, query, keys, values)
+
+
+TILE = 512
+
+
+def project_kernel(rows_ref, weight_ref, out_ref):
+    part = jnp.dot(rows_ref[...], weight_ref[...], preferred_element_type=jnp.float32)
+    out_ref[...] = part.astype(jnp.bfloat16)
+
+
+def project(rows, weight, start, stop):
+    height, depth = rows.shape
+    columns = (stop - start) * TILE
+    return pl.pallas_call(
+        project_kernel,
+        grid=(stop - start,),
+        out_shape=jax.ShapeDtypeStruct((height, columns), rows.dtype),
+        in_specs=[
+            pl.BlockSpec((height, depth), lambda i: (0, 0)),
+            pl.BlockSpec((depth, TILE), lambda i: (0, start + i)),
+        ],
+        out_specs=pl.BlockSpec((height, TILE), lambda i: (0, i)),
+        compiler_params=pltpu.CompilerParams(vmem_limit_bytes=48 * 1024 * 1024),
+        cost_estimate=pl.CostEstimate(
+            flops=2 * height * depth * columns,
+            bytes_accessed=2 * depth * columns,
+            transcendentals=0,
+        ),
+        name="project",
+    )(rows, weight)
 
 
 LEVEL = 4
@@ -249,7 +279,9 @@
             pltpu.SemaphoreType.DMA((count, 2)),
             pltpu.SemaphoreType.DMA((2,)),
         ],
-        compiler_params=pltpu.CompilerParams(collective_id=0, has_side_effects=True),
+        compiler_params=pltpu.CompilerParams(
+            collective_id=0, has_side_effects=True, vmem_limit_bytes=60 * 1024 * 1024
+        ),
         name="gather",
     )(keys, values)
 
@@ -262,29 +294,28 @@
     ids, count, seats = plan(vert_cols, slash_off, doc_ids, context, blocks)
     all_keys, all_values = gather(keys, values, lax.axis_size("context"))
 
-    def projected(rows, weight):
-        return jnp.dot(rows, weight, preferred_element_type=jnp.float32).astype(jnp.bfloat16)
-
     if shares != 2 or blocks % shares:
         first = jnp.zeros((), jnp.int32)
         rows = attend(query, all_keys, all_values, first, 1, ids, count, seats)
         return lax.psum_scatter(
-            projected(rows, out_weight), "tensor", scatter_dimension=0, tiled=True
+            jnp.dot(rows, out_weight, preferred_element_type=jnp.float32).astype(jnp.bfloat16),
+            "tensor",
+            scatter_dimension=0,
+            tiled=True,
         )
     theirs = attend(query, all_keys, all_values, 1 - tensor, shares, ids, count, seats)
-    cuts = 2
-    width = out_weight.shape[1] // cuts
-    moved = []
-    for cut in range(cuts):
-        weight = out_weight[:, cut * width:(cut + 1) * width]
-        moved.append(lax.ppermute(projected(theirs, weight), "tensor", [(0, 1), (1, 0)]))
+    tiles = out_weight.shape[1] // TILE
+    cut = 2
+    moved = [
+        lax.ppermute(project(theirs, out_weight, at, at + cut), "tensor", [(0, 1), (1, 0)])
+        for at in range(0, tiles, cut)
+    ]
     part, _ = lax.optimization_barrier((tensor, theirs))
     mine = attend(query, all_keys, all_values, part, shares, ids, count, seats)
-    outs = []
-    for cut in range(cuts):
-        weight = out_weight[:, cut * width:(cut + 1) * width]
-        outs.append(projected(mine, weight).astype(jnp.float32) + moved[cut].astype(jnp.float32))
-    return jnp.concatenate(outs, axis=1).astype(jnp.bfloat16)
+    own = project(mine, out_weight, 0, tiles)
+    return (
+        own.astype(jnp.float32) + jnp.concatenate(moved, axis=1).astype(jnp.float32)
+    ).astype(jnp.bfloat16)
 
 
 def solution(mesh):

time: 137 us -> 132 us (0.964); the launches traced: 135 us -> 132 us
  Pallas kernels: 93.4 us -> 118 us
  matrix products: 20.8 us -> 0 us
  waiting for transfers between devices: 10.1 us -> 0.01 us
  starting transfers between devices: 1.56 us -> 3.93 us
    pallas_call x0 -> x5, Pallas kernels: none -> 21.4 us  [project(): pl.pallas_call(project_kernel, grid=(stop - start,), out_shape=jax.ShapeD...]
    dot_general x4 -> x0, matrix products: 20.8 us -> none  [projected(): jnp.dot(rows, weight, preferred_element_type=jnp.float32)]
    ppermute x2 -> x4, waiting for transfers between devices: 10.1 us -> 0.01 us  [per_device(): lax.ppermute(project(theirs, out_weight, at, at + cut), 'tensor', [(0, 1)...]
    pallas_call x2, Pallas kernels: 28.1 us -> 31 us  [attend(): pl.pallas_call(functools.partial(attend_kernel, query.shape[0] // BLOCK,...]
    ppermute x2 -> x4, starting transfers between devices: 1.56 us -> 3.93 us  [per_device(): lax.ppermute(project(theirs, out_weight, at, at + cut), 'tensor', [(0, 1)...]
    convert_element_type x0 -> x1, other arithmetic: none -> 1.69 us  [per_device(): return (own.astype(jnp.float32) + jnp.concatenate(moved, axis=1).astype(j...]
  transfers between devices with their start and end apart: 2 -> 4, of which waited for: 1 -> 0; matrix products, arithmetic and copies ran while one was open for 8% -> 0% of each run, Pallas kernels for 10% -> 26%
where the time goes in v3:
time: 132 us
  Pallas kernels  118 us (89%)
  other arithmetic  6.41 us (5%)
  starting transfers between devices  3.93 us (3%)
  local copies, waits for them, and re-layouts  3.33 us (3%)
    pallas_call x1, Pallas kernels, gather(): pl.pallas_call(functools.partial(gather_kernel, levels), out_shape=(shape...  65.4 us
    pallas_call x2, Pallas kernels, attend(): pl.pallas_call(functools.partial(attend_kernel, query.shape[0] // BLOCK,...  31 us
    pallas_call x5, Pallas kernels, project(): pl.pallas_call(project_kernel, grid=(stop - start,), out_shape=jax.ShapeD...  21.4 us
    ppermute x4, starting transfers between devices, per_device(): lax.ppermute(project(theirs, out_weight, at, at + cut), 'tensor', [(0, 1)...  3.93 us
  transfers between devices with their start and end apart: 4, of which 0 were waited for; matrix products, arithmetic and copies ran while one was open for 0% of the time, Pallas kernels for 26%

profile of v3, /device:TPU:27, one launch (start us, length us, event | category | flops | bytes accessed | tf_op | source)
XLA Modules:
  0.0 131.7 jit_solution(9956900706015499552)
XLA Ops:
  0.0 0.7 dynamic_slice.3
  0.8 0.8 convert_reduce_fusion.2
  1.6 0.7 add_select_fusion
  2.3 0.8 copy.8
  3.1 0.8 broadcast_subtract_fusion.1
  3.8 0.8 broadcast_compare_fusion
  4.6 0.1 broadcast_subtract_fusion
  4.7 0.1 compare_reduce_fusion
  4.8 0.1 not_and_fusion
  4.9 0.1 broadcast_in_dim.19
  5.0 0.2 convert_reduce_fusion.1
  5.2 0.1 copy.9
  5.3 0.1 reshape.53.count_ref
  5.4 0.1 broadcast_in_dim.21
  5.5 0.1 pad_add_fusion
  5.6 0.5 convert_reduce_fusion
  6.1 0.5 select_reduce_fusion
  6.5 0.1 fusion.1
  6.6 0.1 select_n.24.ids_ref
  6.7 65.4 %gather.1 = (bf16[6144,512]{1,0:T(8,128)(2,1)}, bf16[6144,512]{1,0:T(8,128)(2,1)}) custom-call(bf16[384,512]{1,0:T(8,128)(2,1)} %k_ref.1, bf16[384,512]{1,0:T(8,128)(2,1)} %v_ref.1), custom_call_target="tpu_custom_call" | custom-call | tf_op jit(solution)/shard_map/gather/pallas_call | solution.py:272
  72.1 0.0 copy-start
  72.1 1.4 %copy-done = bf16[384,2048]{1,0:T(8,128)(2,1)S(1)} copy-done((bf16[384,2048]{1,0:T(8,128)(2,1)S(1)}, bf16[384,2048]{1,0:T(8,128)(2,1)}, u32[]{:S(2)}) %copy-start) | copy-done | bytes 1572888
  73.5 15.0 %attend.2.rows_ref = bf16[192,2048]{1,0:T(8,128)(2,1)S(1)} custom-call(s32[1]{0:T(128)} %bitcast.part_ref, s32[768]{0:T(1024)S(1)} %select_n.24.ids_ref, s32[24]{0:T(128)S(1)} %reshape.53.count_ref, bf16[384,2048]{1,0:T(8,128)(2,1)S(1)} %copy-done, bf16[6144,512]{1,0:T(8,128)(2,1)} %get-tuple-element.8.k_ref, bf16[6144,512]{1,0:T(8,128)(2,1)} %get-tuple-element.9.v_ref), custom_call_target="tpu_custom_call" | custom-call | flops 3221225472 | bytes 12582912 | tf_op jit(solution)/shard_map/attend/pallas_call | solution.py:126
  88.5 2.9 %project.6 = bf16[192,1024]{1,0:T(8,128)(2,1)S(1)} custom-call(bf16[192,2048]{1,0:T(8,128)(2,1)S(1)} %attend.2.rows_ref, bf16[2048,4096]{1,0:T(8,128)(2,1)} %weight_ref.9), custom_call_target="tpu_custom_call" | custom-call | flops 805306368 | bytes 4194304 | tf_op jit(solution)/shard_map/project/pallas_call | solution.py:151
  91.4 2.1 %collective-permute-start = (bf16[192,1024]{1,0:T(8,128)(2,1)S(1)}, bf16[192,1024]{1,0:T(8,128)(2,1)S(1)}, u32[]{:S(2)}, u32[]{:S(2)}) collective-permute-start(bf16[192,1024]{1,0:T(8,128)(2,1)S(1)} %project.6), channel_id=1, source_target_pairs={{0,1},{1,0},{2,3},{3,2},{4,5},{5,4},{6,7},{7,6},{8,9},{9,8},{10,11... | collective-permute-start | bytes 1179656 | tf_op jit(solution)/shard_map/ppermute | solution.py:310
  93.5 2.9 %project.7 = bf16[192,1024]{1,0:T(8,128)(2,1)S(1)} custom-call(bf16[192,2048]{1,0:T(8,128)(2,1)S(1)} %attend.2.rows_ref, bf16[2048,4096]{1,0:T(8,128)(2,1)} %weight_ref.9), custom_call_target="tpu_custom_call" | custom-call | flops 805306368 | bytes 4194304 | tf_op jit(solution)/shard_map/project/pallas_call | solution.py:151
  96.4 0.1 collective-permute-start.1
  96.5 2.9 %project.8 = bf16[192,1024]{1,0:T(8,128)(2,1)S(1)} custom-call(bf16[192,2048]{1,0:T(8,128)(2,1)S(1)} %attend.2.rows_ref, bf16[2048,4096]{1,0:T(8,128)(2,1)} %weight_ref.9), custom_call_target="tpu_custom_call" | custom-call | flops 805306368 | bytes 4194304 | tf_op jit(solution)/shard_map/project/pallas_call | solution.py:151
  99.4 0.0 copy-start.1
  99.4 1.5 %collective-permute-start.2 = (bf16[192,1024]{1,0:T(8,128)(2,1)S(1)}, bf16[192,1024]{1,0:T(8,128)(2,1)S(1)}, u32[]{:S(2)}, u32[]{:S(2)}) collective-permute-start(bf16[192,1024]{1,0:T(8,128)(2,1)S(1)} %project.8), channel_id=1, source_target_pairs={{0,1},{1,0},{2,3},{3,2},{4,5},{5,4},{6,7},{7,6},{8,9},{9,8},{10,11... | collective-permute-start | bytes 1179656 | tf_op jit(solution)/shard_map/ppermute | solution.py:310
  100.9 2.9 %project.9 = bf16[192,1024]{1,0:T(8,128)(2,1)S(1)} custom-call(bf16[192,2048]{1,0:T(8,128)(2,1)S(1)} %attend.2.rows_ref, bf16[2048,4096]{1,0:T(8,128)(2,1)} %weight_ref.9), custom_call_target="tpu_custom_call" | custom-call | flops 805306368 | bytes 4194304 | tf_op jit(solution)/shard_map/project/pallas_call | solution.py:151
  103.8 0.2 collective-permute-start.3
  104.0 0.0 copy-done.1
  104.0 16.1 %attend.3.rows_ref = bf16[192,2048]{1,0:T(8,128)(2,1)S(1)} custom-call(s32[1]{0:T(128)} %bitcast.1.part_ref, s32[768]{0:T(1024)S(1)} %select_n.24.ids_ref, s32[24]{0:T(128)S(1)} %reshape.53.count_ref, bf16[384,2048]{1,0:T(8,128)(2,1)S(1)} %copy-done.1, bf16[6144,512]{1,0:T(8,128)(2,1)} %get-tuple-element.8.k_ref, bf16[6144,512]{1,0:T(8,128)(2,1)} %get-tuple-element.9.v_ref), custom_call_target="tpu_custom_call" | custom-call | flops 3221225472 | bytes 12582912 | tf_op jit(solution)/shard_map/attend/pallas_call | solution.py:126
  120.0 10.0 %project.5 = bf16[192,4096]{1,0:T(8,128)(2,1)S(1)} custom-call(bf16[192,2048]{1,0:T(8,128)(2,1)S(1)} %attend.3.rows_ref, bf16[2048,4096]{1,0:T(8,128)(2,1)} %weight_ref.9), custom_call_target="tpu_custom_call" | custom-call | flops 3221225472 | bytes 16777216 | tf_op jit(solution)/shard_map/project/pallas_call | solution.py:151
  130.0 0.0 collective-permute-done
  130.0 0.0 collective-permute-done.1
  130.0 0.0 collective-permute-done.2
  130.0 0.0 collective-permute-done.3
  130.0 1.7 %add_convert_fusion = bf16[192,4096]{1,0:T(8,128)(2,1)} fusion(bf16[192,4096]{1,0:T(8,128)(2,1)S(1)} %project.5, bf16[192,1024]{1,0:T(8,128)(2,1)S(1)} %collective-permute-done.3, bf16[192,1024]{1,0:T(8,128)(2,1)S(1)} %collective-permute-done.2, bf16[192,1024]{1,0:T(8,128)(2,1)S(1)} %collective-permute-done.1, bf16[192,1024]{1,0:T(8,128)(2,1)S(1)} %collective-permute-done), kind=kLoop, calls=%fused_computation | loop fusion | flops 8650752 | bytes 4718592 | tf_op jit(solution)/shard_map/convert_element_type | solution.py:318
  (6 shorter events, 0.0 us)
Async XLA Ops:
  72.1 1.4 %copy-start = (bf16[384,2048]{1,0:T(8,128)(2,1)S(1)}, bf16[384,2048]{1,0:T(8,128)(2,1)}, u32[]{:S(2)}) copy-start(bf16[384,2048]{1,0:T(8,128)(2,1)} %q_ref.3) | copy-start | bytes 4718596
  91.4 38.6 %collective-permute-start = (bf16[192,1024]{1,0:T(8,128)(2,1)S(1)}, bf16[192,1024]{1,0:T(8,128)(2,1)S(1)}, u32[]{:S(2)}, u32[]{:S(2)}) collective-permute-start(bf16[192,1024]{1,0:T(8,128)(2,1)S(1)} %project.6), channel_id=1, source_target_pairs={{0,1},{1,0},{2,3},{3,2},{4,5},{5,4},{6,7},{7,6},{8,9},{9,8},{10,11... | collective-permute-start | bytes 1179656 | tf_op jit(solution)/shard_map/ppermute | solution.py:310
  96.4 33.6 %collective-permute-start.1 = (bf16[192,1024]{1,0:T(8,128)(2,1)S(1)}, bf16[192,1024]{1,0:T(8,128)(2,1)S(1)}, u32[]{:S(2)}, u32[]{:S(2)}) collective-permute-start(bf16[192,1024]{1,0:T(8,128)(2,1)S(1)} %project.7), channel_id=1, source_target_pairs={{0,1},{1,0},{2,3},{3,2},{4,5},{5,4},{6,7},{7,6},{8,9},{9,8},{10,11... | collective-permute-start | bytes 1179656 | tf_op jit(solution)/shard_map/ppermute | solution.py:310
  99.4 4.6 %copy-start.1 = (bf16[384,2048]{1,0:T(8,128)(2,1)S(1)}, bf16[384,2048]{1,0:T(8,128)(2,1)}, u32[]{:S(2)}) copy-start(bf16[384,2048]{1,0:T(8,128)(2,1)} %q_ref.3) | copy-start | bytes 4718596
  99.4 30.6 %collective-permute-start.2 = (bf16[192,1024]{1,0:T(8,128)(2,1)S(1)}, bf16[192,1024]{1,0:T(8,128)(2,1)S(1)}, u32[]{:S(2)}, u32[]{:S(2)}) collective-permute-start(bf16[192,1024]{1,0:T(8,128)(2,1)S(1)} %project.8), channel_id=1, source_target_pairs={{0,1},{1,0},{2,3},{3,2},{4,5},{5,4},{6,7},{7,6},{8,9},{9,8},{10,11... | collective-permute-start | bytes 1179656 | tf_op jit(solution)/shard_map/ppermute | solution.py:310
  103.8 26.2 %collective-permute-start.3 = (bf16[192,1024]{1,0:T(8,128)(2,1)S(1)}, bf16[192,1024]{1,0:T(8,128)(2,1)S(1)}, u32[]{:S(2)}, u32[]{:S(2)}) collective-permute-start(bf16[192,1024]{1,0:T(8,128)(2,1)S(1)} %project.9), channel_id=1, source_target_pairs={{0,1},{1,0},{2,3},{3,2},{4,5},{5,4},{6,7},{7,6},{8,9},{9,8},{10,11... | collective-permute-start | bytes 1179656 | tf_op jit(solution)/shard_map/ppermute | solution.py:310
